TPU v7x, 128 devices: a whole 4x4x4 slice. The times are simulated.
128 devices in a mesh: node: 8 (over z, core), local: 16 (over x, y).
Axes of the slice: x: 4, y: 4, z: 4, core: 2. Of those that a mesh axis runs over, the one named last changes fastest.
Arguments:
- activations: bfloat16 [1024, 7168], P(('node', 'local')), may hold values from -6 to 6
- expert_ids: int32 [1024, 8], P(('node', 'local')), may hold values from 0 to 31, all different within a row; in each aligned block of 8 rows (0 to 7, 8 to 15, ...) at most 4 rows name the same one
- route_weights: bfloat16 [1024, 8], P(('node', 'local')), may hold values from 0.099609375 to 0.5
- w_gate: bfloat16 [32, 7168, 2048], P('local', None, 'node'), may hold values from -0.0625 to 0.0625
- w_up: bfloat16 [32, 7168, 2048], P('local', None, 'node'), may hold values from -0.0625 to 0.0625
- w_down: bfloat16 [32, 2048, 7168], P('local', 'node'), may hold values from -0.125 to 0.125
Outputs:
- combined: bfloat16 [1024, 7168], P(('node', 'local'))
Inputs may be any that keep to these rules, and one draw needn't show every extreme that they name: `expert_ids`: each row names 8 different experts. Among the 8 rows of one device no expert is named by more than 4 rows, a bound that some block reaches.
All inputs are finite; a program needn't handle non-finite values.
Results may differ from a plain program's by a relative error of at most 0.02.
Values may be sent and summed in bfloat16 or wider, within the bound.
A program may use at most 192 MiB of HBM per device.

v0:
```python
import jax
import jax.numpy as jnp
from jax import lax
from jax.sharding import PartitionSpec as P


def place_slots(expert_ids, route_weights, experts, capacity):
    flat_ids = expert_ids.reshape(-1)
    count = flat_ids.shape[0]
    top_count = expert_ids.shape[1]
    onehot = (flat_ids[:, None] == jnp.arange(experts, dtype=jnp.int32)[None, :]).astype(jnp.int32)
    before = jnp.cumsum(onehot, axis=0) - onehot
    ranks = jnp.sum(before * onehot, axis=1)
    slots = flat_ids * capacity + ranks
    source = (
        jnp.zeros((experts * capacity,), jnp.int32)
        .at[slots]
        .set(jnp.arange(count, dtype=jnp.int32) // top_count)
    )
    filled = (
        jnp.zeros((experts * capacity,), jnp.bfloat16)
        .at[slots]
        .set(jnp.ones((count,), jnp.bfloat16))
    )
    slot_weights = (
        jnp.zeros((experts * capacity,), jnp.bfloat16).at[slots].set(route_weights.reshape(-1))
    )
    return (slots, source, filled, slot_weights)


def expert_apply(received, w_gate, w_up, w_down):
    features, weights = received
    gate = jnp.einsum("secd,edf->secf", features, w_gate, preferred_element_type=jnp.float32)
    up = jnp.einsum("secd,edf->secf", features, w_up, preferred_element_type=jnp.float32)
    hidden = (jax.nn.silu(gate) * up).astype(jnp.bfloat16)
    partial_out = jnp.einsum("secf,efd->secd", hidden, w_down, preferred_element_type=jnp.float32)
    return (partial_out * weights.astype(jnp.float32)[..., None]).astype(jnp.bfloat16)


def body(activations, expert_ids, route_weights, w_gate, w_up, w_down):
    tok_rows = activations.shape[0]
    width = activations.shape[1]
    top_count = expert_ids.shape[1]
    n_node = lax.axis_size("node")
    n_local = lax.axis_size("local")
    exp_local = w_gate.shape[0]
    experts = exp_local * n_local
    most_rows = tok_rows // 2
    rail_act, rail_ids, rail_weights = (
        lax.all_gather(activations, "node", axis=0, tiled=True),
        lax.all_gather(expert_ids, "node", axis=0, tiled=True),
        lax.all_gather(route_weights, "node", axis=0, tiled=True),
    )
    capacity = n_node * most_rows
    slots, source, filled, slot_weights = place_slots(rail_ids, rail_weights, experts, capacity)
    buffer = rail_act[source] * filled[:, None]
    buffer = buffer.reshape(n_local, exp_local, capacity, width)
    slot_weights = slot_weights.reshape(n_local, exp_local, capacity)
    contrib = expert_apply(
        (
            lax.all_to_all(buffer, "local", split_axis=0, concat_axis=0, tiled=True),
            lax.all_to_all(slot_weights, "local", split_axis=0, concat_axis=0, tiled=True),
        ),
        w_gate,
        w_up,
        w_down,
    )
    returned = lax.all_to_all(contrib, "local", split_axis=0, concat_axis=0, tiled=True)
    picked = returned.reshape(experts * capacity, width)[slots].astype(jnp.float32)
    summed = jnp.sum(picked.reshape(n_node * tok_rows, top_count, width), axis=1)
    combined = lax.psum_scatter(
        summed.astype(jnp.bfloat16), "node", scatter_dimension=0, tiled=True
    )
    return combined


def solution(mesh):
    return jax.shard_map(
        body,
        mesh=mesh,
        in_specs=(
            P(("node", "local"), None),
            P(("node", "local"), None),
            P(("node", "local"), None),
            P("local", None, "node"),
            P("local", None, "node"),
            P("local", "node", None),
        ),
        out_specs=P(("node", "local"), None),
        check_vma=False,
    )
```

profile of v0, /device:TPU:1, one launch (start us, length us, event | category | flops | bytes accessed | tf_op | source)
XLA Modules:
  0.0 740.0 jit_solution(8976949094551524236)
XLA Ops:
  6.5 15.4 %all_gather.10 = s32[64,8]{1,0:T(8,128)S(1)} all-gather(s32[8,8]{1,0:T(8,128)} %param.7), channel_id=1, replica_groups=mesh['node'=8,'local'=16] {'node'}, dimensions={0}, use_global_device_ids=true | all-gather | bytes 2304 | tf_op jit(solution)/shard_map/all_gather | solution.py:51
  22.0 0.1 eq.29
  22.1 0.1 eq.25
  22.2 1.2 reduce-window.6
  23.4 0.2 slice_reduce_fusion
  23.6 0.1 mul.47
  23.7 11.4 %all_gather.11 = bf16[64,8]{1,0:T(8,128)(2,1)S(1)} all-gather(bf16[8,8]{1,0:T(8,128)(2,1)} %param.8), channel_id=1, replica_groups=mesh['node'=8,'local'=16] {'node'}, dimensions={0}, use_global_device_ids=true | all-gather | bytes 1152 | tf_op jit(solution)/shard_map/all_gather | solution.py:52
  35.1 0.1 reshape.106
  35.2 0.1 fusion.30
  35.3 3.8 scatter_custom_fusion.2
  39.1 0.7 reshape.68
  39.8 6.8 all-to-all-start.1
  46.5 2.4 scatter_custom_fusion
  49.0 14.1 %all_gather.9 = bf16[64,7168]{1,0:T(8,128)(2,1)S(1)} all-gather(bf16[8,7168]{1,0:T(8,128)(2,1)} %param.6), channel_id=1, replica_groups=mesh['node'=8,'local'=16] {'node'}, dimensions={0}, use_global_device_ids=true | all-gather | bytes 1032192 | tf_op jit(solution)/shard_map/all_gather | solution.py:50
  63.1 3.8 scatter_custom_fusion.1
  66.8 0.1 mul.49
  66.9 11.5 %gather_fusion = bf16[1024,7168]{1,0:T(8,128)(2,1)} fusion(bf16[64,7168]{1,0:T(8,128)(2,1)S(1)} %all_gather.9, s32[1024]{0:T(1024)S(1)} %fusion.32), kind=kCustom, calls=%fused_computation | custom fusion | bytes 29364224 | tf_op jit(solution)/shard_map/gather | solution.py:56
  78.4 13.4 %broadcast_multiply_fusion = bf16[16,2,32,7168]{3,2,1,0:T(8,128)(2,1)} fusion(bf16[16,2,32,7168]{3,2,1,0:T(8,128)(2,1)} %bitcast.61, bf16[16,2,32]{2,1,0:T(2,128)(2,1)S(1)} %mul.49), kind=kLoop, calls=%fused_computation.15 | loop fusion | flops 7340032 | bytes 29362176 | tf_op jit(solution)/shard_map/mul | solution.py:56
  91.8 0.0 all-to-all-done.1
  91.8 7.0 all-to-all-start
  98.8 257.1 %all-to-all-done = bf16[16,2,32,7168]{3,2,1,0:T(8,128)(2,1)} async-done(((bf16[16,2,32,7168]{3,2,1,0:T(8,128)(2,1)}), bf16[16,2,32,7168]{3,2,1,0:T(8,128)(2,1)}, u32[]{:S(2)}, u32[]{:S(2)}) %all-to-all-start) | async-done | bytes 14680096 | tf_op jit(solution)/shard_map/all_to_all | solution.py:61
  355.9 9.3 %fusion.8 = f32[16,2,32,256]{3,2,0,1:T(8,128)S(1)} fusion(bf16[2,7168,256]{2,1,0:T(8,128)(2,1)} %param.9, bf16[16,2,32,7168]{3,2,1,0:T(8,128)(2,1)} %all-to-all-done), kind=kOutput, calls=%fused_computation.16 | convolution fusion | flops 3758096384 | bytes 23068672 | tf_op jit(solution)/shard_map/secd,edf->secf/dot_general | solution.py:33
  365.2 11.4 %fusion.23 = bf16[16,2,32,256]{3,2,0,1:T(8,128)(2,1)S(1)} fusion(bf16[2,7168,256]{2,1,0:T(8,128)(2,1)} %param.10, bf16[16,2,32,7168]{3,2,1,0:T(8,128)(2,1)} %all-to-all-done, f32[16,2,32,256]{3,2,0,1:T(8,128)S(1)} %fusion.8), kind=kOutput, calls=%fused_computation.19 | convolution fusion | flops 3759669248 | bytes 23592960 | tf_op jit(solution)/shard_map/secd,edf->secf/dot_general | solution.py:34
  376.6 10.4 %fusion = bf16[16,2,32,7168]{3,2,0,1:T(8,128)(2,1)} fusion(bf16[16,2,32,256]{3,2,0,1:T(8,128)(2,1)S(1)} %fusion.23, f32[16,2,32]{2,0,1:T(8,128)S(1)} %copy_convert_fusion, bf16[2,256,7168]{2,1,0:T(8,128)(2,1)} %param.11), kind=kOutput, calls=%fused_computation.6 | convolution fusion | flops 3772776448 | bytes 22548480 | tf_op jit(solution)/shard_map/secf,efd->secd/dot_general | solution.py:36
  387.0 13.6 %copy.26 = bf16[16,2,32,7168]{3,2,1,0:T(8,128)(2,1)} copy(bf16[16,2,32,7168]{3,2,0,1:T(8,128)(2,1)} %fusion) | data formatting | bytes 29360128 | tf_op jit(solution)/shard_map/convert_element_type | solution.py:37
  400.6 8.5 %all-to-all-start.2 = ((bf16[16,2,32,7168]{3,2,1,0:T(8,128)(2,1)}), bf16[16,2,32,7168]{3,2,1,0:T(8,128)(2,1)}, u32[]{:S(2)}, u32[]{:S(2)}) async-start(bf16[16,2,32,7168]{3,2,1,0:T(8,128)(2,1)} %copy.26), calls=%async_computation.2 | async-start | bytes 29360128 | tf_op jit(solution)/shard_map/all_to_all | solution.py:68
  409.1 0.0 reduce-scatter.2.cloned.1.call-start
  409.2 257.4 %all-to-all-done.2 = bf16[16,2,32,7168]{3,2,1,0:T(8,128)(2,1)} async-done(((bf16[16,2,32,7168]{3,2,1,0:T(8,128)(2,1)}), bf16[16,2,32,7168]{3,2,1,0:T(8,128)(2,1)}, u32[]{:S(2)}, u32[]{:S(2)}) %all-to-all-start.2) | async-done | bytes 14680096 | tf_op jit(solution)/shard_map/all_to_all | solution.py:68
  666.5 21.1 %gather_fusion.1 = bf16[512,7168]{1,0:T(8,128)(2,1)} fusion(bf16[1024,7168]{1,0:T(8,128)(2,1)} %bitcast.13, s32[1024]{0:T(1024)S(1)} %pad_clamp_fusion), kind=kCustom, calls=%fused_computation.1 | custom fusion | bytes 14682112 | tf_op jit(solution)/shard_map/gather | solution.py:69
  687.6 8.9 %bitcast_reduce_fusion = bf16[64,7168]{1,0:T(8,128)(2,1)} fusion(bf16[512,7168]{1,0:T(8,128)(2,1)} %gather_fusion.1), kind=kLoop, calls=%fused_computation.14 | loop fusion | flops 3211264 | bytes 8257536 | tf_op jit(solution)/shard_map/reduce_sum | solution.py:70
  696.6 0.0 reduce-scatter.2.cloned.1.call-update
  696.6 36.6 %reduce-scatter.2.cloned.1.call-done = bf16[8,7168]{1,0:T(8,128)(2,1)} async-done(((bf16[64,7168]{1,0:T(8,128)(2,1)}), bf16[8,7168]{1,0:T(8,128)(2,1)}) %reduce-scatter.2.cloned.1.call-update) | async-done | bytes 114704 | tf_op jit(solution)/shard_map/reduce_scatter | solution.py:71
  (10 shorter events, 0.1 us)
Async XLA Ops:
  39.8 52.0 %all-to-all-start.1 = ((bf16[16,2,32]{2,1,0:T(2,128)(2,1)}), bf16[16,2,32]{2,1,0:T(2,128)(2,1)S(1)}, u32[]{:S(2)}, u32[]{:S(2)}) async-start(bf16[16,2,32]{2,1,0:T(2,128)(2,1)} %reshape.68), calls=%async_computation.1 | async-start | bytes 16384 | tf_op jit(solution)/shard_map/all_to_all | solution.py:62
  91.8 264.1 %all-to-all-start = ((bf16[16,2,32,7168]{3,2,1,0:T(8,128)(2,1)}), bf16[16,2,32,7168]{3,2,1,0:T(8,128)(2,1)}, u32[]{:S(2)}, u32[]{:S(2)}) async-start(bf16[16,2,32,7168]{3,2,1,0:T(8,128)(2,1)} %broadcast_multiply_fusion), calls=%async_computation | async-start | bytes 29360128 | tf_op jit(solution)/shard_map/all_to_all | solution.py:61
  400.6 265.9 %all-to-all-start.2 = ((bf16[16,2,32,7168]{3,2,1,0:T(8,128)(2,1)}), bf16[16,2,32,7168]{3,2,1,0:T(8,128)(2,1)}, u32[]{:S(2)}, u32[]{:S(2)}) async-start(bf16[16,2,32,7168]{3,2,1,0:T(8,128)(2,1)} %copy.26), calls=%async_computation.2 | async-start | bytes 29360128 | tf_op jit(solution)/shard_map/all_to_all | solution.py:68
  409.1 324.0 %reduce-scatter.2.cloned.1.call-start = ((), (), s32[]{:S(2)}) async-start(), calls=%async_computation.4 | async-start | bytes 1032192 | tf_op jit(solution)/shard_map/reduce_scatter | solution.py:71
Sparse Core Ops, SparseCore 0:
  696.7 36.3 reduce-scatter.1
where the time goes:
time: 743 us; the launch traced here: 740 us
  waiting for transfers between devices  551 us (74%)
  local copies, waits for them, and re-layouts  57.5 us (8%)
  blocking collectives  40.9 us (6%)
  matrix products  31.1 us (4%)
  other arithmetic  23.7 us (3%)
  starting transfers between devices  22.3 us (3%)
  between operations  13.5 us (2%)
    all_to_all x1, waiting for transfers between devices, body(): lax.all_to_all(contrib, 'local', split_axis=0, concat_axis=0, tiled=True)  257 us
    all_to_all x1, waiting for transfers between devices, body(): lax.all_to_all(buffer, 'local', split_axis=0, concat_axis=0, tiled=True)  257 us
    reduce_scatter x1, waiting for transfers between devices, body(): lax.psum_scatter(summed.astype(jnp.bfloat16), 'node', scatter_dimension=0...  36.6 us
    gather x1, local copies, waits for them, and re-layouts, body(): returned.reshape(experts * capacity, width)[slots].astype(jnp.float32)  21.1 us
    all_gather x1, blocking collectives, body(): lax.all_gather(expert_ids, 'node', axis=0, tiled=True)  15.4 us
  transfers between devices with their start and end apart: 4, of which 3 were waited for; matrix products, arithmetic and copies ran while one was open for 4% of the time, Pallas kernels for 0%

commit v1 on v0

v1 whole, which is shorter than its diff:
```python
import jax
import jax.numpy as jnp
from jax import lax
from jax.experimental import pallas as pl
from jax.experimental.pallas import tpu as pltpu
from jax.sharding import PartitionSpec as P

MESH = pl.DeviceIdType.MESH
F32 = jnp.float32
BF16 = jnp.bfloat16

SIDE = 4
ROWS = 16
HALF = 3584
EXTRA = 128
FFS = 256
PARTS = (
    ((0, 1, 2), 0, 1280, 1280),
    ((1, 2, 0), 1280, 1280, 1280),
    ((2, 0, 1), 2560, 1024, 1152),
)


def kernel(
    x_in, ids_in, rw_in, wg_hbm, wu_hbm, wd_hbm, out_ref,
    pack, pack_got, xb0, xb1, xb2, wgu, wd, acc, hb,
    ob0, ob1, ob2, ro0, ro1, ro2, rp0, rp1, rp2, rm0, rm1, rm2,
    bo0, bo1, bo2, bp0, bp1, bp2, bm0, bm1, bm2, ra0, ra1, ra2,
    fin, fin_got, ssem, rsem, lsem,
):
    node = lax.axis_index("node")
    local = lax.axis_index("local")
    core = lax.rem(node, 2)
    me = (local // SIDE, lax.rem(local, SIDE), node // 2)
    mate = 1 - core
    xb, ob = (xb0, xb1, xb2), (ob0, ob1, ob2)
    ro, rp, rm = (ro0, ro1, ro2), (rp0, rp1, rp2), (rm0, rm1, rm2)
    bo, bp, bm, ra = (bo0, bo1, bo2), (bp0, bp1, bp2), (bm0, bm1, bm2), (ra0, ra1, ra2)

    def off(d, k):
        return lax.rem(me[d] + k, SIDE)

    def device(d=None, k=0, other_core=False):
        at = [off(i, k) if i == d else me[i] for i in range(3)]
        return (at[2] * 2 + (mate if other_core else core), at[0] * SIDE + at[1])

    def ix(*pairs):
        at = [slice(None)] * 3
        for d, v in pairs:
            at[d] = v
        return tuple(at)

    copies = []

    def send(src, dst, to):
        n = len(copies)
        cp = pltpu.make_async_remote_copy(
            src_ref=src, dst_ref=dst, send_sem=ssem.at[n], recv_sem=rsem.at[n], device_id=to, device_id_type=MESH
        )
        cp.start()
        copies.append(cp)
        return cp

    loads = []
    for e in range(2):
        for g, w in enumerate((wg_hbm, wu_hbm)):
            for h in range(2):
                n = len(loads)
                cp = pltpu.make_async_copy(w.at[e, pl.ds(h * HALF, HALF)], wgu.at[2 * e + g, h], lsem.at[n])
                cp.start()
                loads.append(cp)
    own_cols = pl.ds(pl.multiple_of(core * HALF, 128), HALF)
    mate_cols = pl.ds(pl.multiple_of(mate * HALF, 128), HALF)
    cp = pltpu.make_async_copy(wd_hbm.at[:, :, own_cols], wd.at[core], lsem.at[len(loads)])
    cp.start()
    loads.append(cp)

    barrier = pltpu.get_barrier_semaphore()
    peers = [device(other_core=True)] + [device(d, k) for d in range(3) for k in (1, 2, 3)]
    for peer in peers:
        pl.semaphore_signal(barrier, inc=1, device_id=peer, device_id_type=MESH)

    lane = lax.broadcasted_iota(jnp.int32, (8, EXTRA), 1)
    dense = jnp.zeros((8, EXTRA), F32)
    ids = ids_in[...]
    rw = rw_in[...].astype(F32)
    for k in range(8):
        dense = dense + jnp.where(ids[:, k : k + 1] == lane, rw[:, k : k + 1], 0.0)
    for h in range(2):
        pack[h, :, 0:HALF] = x_in[:, h * HALF : (h + 1) * HALF].astype(F32)
        pack[h, :, HALF : HALF + EXTRA] = dense

    pl.semaphore_wait(barrier, len(peers))
    sister = device(other_core=True)
    swap = send(pack.at[mate], pack_got, sister)
    wd_cp = send(wd_hbm.at[:, :, mate_cols], wd.at[core], sister)
    acc[...] = jnp.zeros_like(acc)
    swap.wait_recv()
    mine, got = pack[core], pack_got[...]
    first = core == 0
    block = jnp.concatenate([jnp.where(first, mine, got), jnp.where(first, got, mine)], axis=0).astype(BF16)
    for p, (_, c0, _, width) in enumerate(PARTS):
        xb[p][core, me[0], me[1], me[2]] = block[:, c0 : c0 + width]

    def gather(p, at, to):
        ref = xb[p].at[(core,) + at]
        return send(ref, ref, to)

    first_hop = []
    for p, ((a, b, c), *_) in enumerate(PARTS):
        at = ix((a, me[a]), (b, me[b]), (c, me[c]))
        first_hop.append([gather(p, at, device(a, k)) for k in (1, 3, 2)])
    line, plane_own, mate_parts = [], [], []
    for p, ((a, b, c), *_) in enumerate(PARTS):
        for cp in first_hop[p]:
            cp.wait_recv()
        at = ix((b, me[b]), (c, me[c]))
        line.append([gather(p, at, device(b, k)) for k in (1, 3)])
        plane_own.append([gather(p, at, device(c, k)) for k in (1, 3)])
        mate_parts.append([gather(p, at, sister)])
    line_far, plane_side = [], []
    for p, ((a, b, c), *_) in enumerate(PARTS):
        up, down = line[p]
        up.wait_recv()
        far = [gather(p, ix((a, pl.ds(0, 2)), (b, off(b, 3)), (c, me[c])), device(b, 1))]
        down.wait_recv()
        far.append(gather(p, ix((a, pl.ds(2, 2)), (b, off(b, 1)), (c, me[c])), device(b, 3)))
        line_far.append(far)
        side = []
        for k in (1, 3):
            at = ix((b, off(b, k)), (c, me[c]))
            side.append([gather(p, at, device(c, j)) for j in (1, 3)])
            mate_parts[p].append(gather(p, at, sister))
        plane_side.append(side)
    plane_far = []
    for p, ((a, b, c), *_) in enumerate(PARTS):
        for cp in line_far[p]:
            cp.wait_recv()
        at = ix((b, off(b, 2)), (c, me[c]))
        plane_far.append([gather(p, at, device(c, j)) for j in (1, 3)])
        mate_parts[p].append(gather(p, at, sister))

    def gate_up(p, h, ci):
        (_, _, c), c0, cols, _ = PARTS[p]
        at = ix((c, ci))

        def one(m, carry):
            x = xb[p][(h,) + at + (slice(None), slice(0, cols))].reshape(256, cols)
            w = wgu[m, h, c0 : c0 + cols]
            r = jnp.dot(x, w, preferred_element_type=F32)
            acc[(m,) + at] += r.reshape(SIDE, SIDE, ROWS, FFS)
            return carry

        lax.fori_loop(0, 4, one, 0)

    opposite = [[] for _ in PARTS]
    for p, ((a, b, c), *_) in enumerate(PARTS):
        up, down = plane_own[p]
        up.wait_recv()
        opposite[p].append(gather(p, ix((b, me[b]), (c, off(c, 3))), device(c, 1)))
        down.wait_recv()
    for cp in loads:
        cp.wait()
    for p, ((a, b, c), *_) in enumerate(PARTS):
        gate_up(p, core, me[c])
    for p, ((a, b, c), *_) in enumerate(PARTS):
        for k, (up, down) in zip((1, 3), plane_side[p]):
            up.wait_recv()
            down.wait_recv()
            if k == 1:
                opposite[p].append(gather(p, ix((b, off(b, 1)), (c, off(c, 3))), device(c, 1)))
            else:
                opposite[p].append(gather(p, ix((b, off(b, 3)), (c, off(c, 1))), device(c, 3)))
    for p, ((a, b, c), *_) in enumerate(PARTS):
        for cp in mate_parts[p]:
            cp.wait_recv()
        gate_up(p, mate, me[c])
    mate_side = [[] for _ in PARTS]
    for p, ((a, b, c), *_) in enumerate(PARTS):
        up, down = plane_far[p]
        down.wait_recv()
        opposite[p].append(gather(p, ix((b, off(b, 2)), (c, off(c, 1))), device(c, 3)))
        up.wait_recv()
        for k in (1, 3):
            mate_side[p].append(gather(p, ix((c, off(c, k))), sister))
    for p, ((a, b, c), *_) in enumerate(PARTS):
        for k in (1, 3):
            gate_up(p, core, off(c, k))
    for p, ((a, b, c), *_) in enumerate(PARTS):
        for k, cp in zip((1, 3), mate_side[p]):
            cp.wait_recv()
            gate_up(p, mate, off(c, k))
    mate_far = []
    for p, ((a, b, c), *_) in enumerate(PARTS):
        for cp in opposite[p]:
            cp.wait_recv()
        mate_far.append(gather(p, ix((c, off(c, 2))), sister))
    for p, ((a, b, c), *_) in enumerate(PARTS):
        gate_up(p, core, off(c, 2))
    for p, ((a, b, c), *_) in enumerate(PARTS):
        mate_far[p].wait_recv()
        gate_up(p, mate, off(c, 2))

    expert = lax.broadcasted_iota(jnp.int32, (256, EXTRA), 1) - local * 2
    hidden_cp = []
    for i in range(SIDE):
        dense = xb2[core, i, :, :, :, 1024:1152].reshape(256, EXTRA).astype(F32)
        for e in range(2):
            weight = jnp.sum(jnp.where(expert == e, dense, 0.0), axis=1, keepdims=True)
            gate = acc[2 * e, i].reshape(256, FFS)
            up = acc[2 * e + 1, i].reshape(256, FFS)
            hidden = gate / (1.0 + jnp.exp(-gate)) * up * weight
            hb[core, i, :, :, :, e * FFS : (e + 1) * FFS] = hidden.astype(BF16).reshape(SIDE, SIDE, ROWS, FFS)
        hidden_cp.append(send(hb.at[core, i], hb.at[core, i], sister))
    wd_cp.wait_recv()
    for cp in hidden_cp:
        cp.wait_recv()

    def project(p, ci):
        (_, _, c), c0, cols, _ = PARTS[p]
        at = ix((c, ci))

        def one(n, carry):
            h0 = hb[(0,) + at].reshape(256, 2 * FFS)
            h1 = hb[(1,) + at].reshape(256, 2 * FFS)
            h = jnp.concatenate([h0, h1], axis=1)
            w = wd[:, :, :, pl.ds(pl.multiple_of(c0 + n * 256, 256), 256)].reshape(4 * FFS, 256)
            r = jnp.dot(h, w, preferred_element_type=F32).astype(BF16)
            ob[p][at + (slice(None), pl.ds(pl.multiple_of(n * 256, 256), 256))] = r.reshape(SIDE, SIDE, ROWS, 256)
            return carry

        lax.fori_loop(0, cols // 256, one, 0)

    def add(dst, dst_at, *others):
        total = dst[dst_at].astype(F32)
        for ref, at in others:
            total = total + ref[at].astype(F32)
        dst[dst_at] = total.astype(BF16)

    far_cp, side_cp = [], [[None] * 8 for _ in PARTS]
    for p, ((a, b, c), *_) in enumerate(PARTS):
        project(p, off(c, 2))
        cps = []
        for k in (2, 1, 3, 0):
            to = 1 if k in (2, 1) else 3
            at = ix((b, off(b, k)), (c, off(c, 2)))
            cps.append(send(ob[p].at[at], ro[p].at[off(b, k)], device(c, to)))
        far_cp.append(cps)
    for p, ((a, b, c), *_) in enumerate(PARTS):
        for s, into in ((1, rp), (3, rm)):
            project(p, off(c, s))
            for k in (3, 0) if s == 1 else (2, 1):
                at = ix((b, off(b, k)), (c, off(c, s)))
                side_cp[p][(0 if s == 1 else 4) + k] = send(ob[p].at[at], into[p].at[off(b, k)], device(c, s))
    for p, ((a, b, c), *_) in enumerate(PARTS):
        project(p, me[c])
    for pair in range(2):
        for p, ((a, b, c), *_) in enumerate(PARTS):
            for s, into in ((1, rp), (3, rm)):
                k = ((2, 1) if s == 1 else (3, 0))[pair]
                far_cp[p][(2, 1, 3, 0).index(k)].wait_recv()
                at = ix((b, off(b, k)), (c, off(c, s)))
                add(ob[p], at, (ro[p], off(b, k)))
                side_cp[p][(0 if s == 1 else 4) + k] = send(ob[p].at[at], into[p].at[off(b, k)], device(c, s))
    low, high = pl.ds(0, 2), pl.ds(2, 2)
    line_opp, line_cp = [None] * 3, [[] for _ in PARTS]
    for k in (2, 3, 1, 0):
        for p, ((a, b, c), *_) in enumerate(PARTS):
            side_cp[p][k].wait_recv()
            side_cp[p][4 + k].wait_recv()
            add(ob[p], ix((b, off(b, k)), (c, me[c])), (rp[p], off(b, k)), (rm[p], off(b, k)))

            def part_of(h, k=k, a=a, b=b, c=c):
                return ix((a, h), (b, off(b, k)), (c, me[c]))

            if k == 2:
                line_opp[p] = (
                    send(ob[p].at[part_of(low)], bo[p].at[low], device(b, 1)),
                    send(ob[p].at[part_of(high)], bo[p].at[high], device(b, 3)),
                )
            elif k == 1:
                line_cp[p].append(send(ob[p].at[part_of(high)], bp[p].at[high], device(b, 1)))
                line_opp[p][0].wait_recv()
                add(ob[p], part_of(low), (bo[p], low))
                line_cp[p].append(send(ob[p].at[part_of(low)], bp[p].at[low], device(b, 1)))
            elif k == 3:
                line_cp[p].append(send(ob[p].at[part_of(low)], bm[p].at[low], device(b, 3)))
                line_opp[p][1].wait_recv()
                add(ob[p], part_of(high), (bo[p], high))
                line_cp[p].append(send(ob[p].at[part_of(high)], bm[p].at[high], device(b, 3)))
    last = [[] for _ in PARTS]
    for p, ((a, b, c), *_) in enumerate(PARTS):
        for cp in line_cp[p]:
            cp.wait_recv()
        add(ob[p], ix((b, me[b]), (c, me[c])), (bp[p], slice(None)), (bm[p], slice(None)))
        for k in (1, 2, 3):
            at = ix((a, off(a, k)), (b, me[b]), (c, me[c]))
            last[p].append(send(ob[p].at[at], ra[p].at[k - 1], device(a, k)))
    for p, ((a, b, c), c0, cols, _) in enumerate(PARTS):
        total = ob[p][me].astype(F32)
        for k in (1, 2, 3):
            last[p][k - 1].wait_recv()
            total = total + ra[p][k - 1].astype(F32)
        fin[0, :, c0 : c0 + cols] = total[0:8]
        fin[1, :, c0 : c0 + cols] = total[8:16]
    final = send(fin.at[mate], fin_got, sister)
    final.wait_recv()
    mine, got = fin[core], fin_got[...]
    out_ref[:, 0:HALF] = jnp.where(first, mine, got).astype(BF16)
    out_ref[:, HALF : 2 * HALF] = jnp.where(first, got, mine).astype(BF16)
    for cp in copies:
        cp.wait_send()


N_COPIES = 170


def body(activations, expert_ids, route_weights, w_gate, w_up, w_down):
    rows, width = activations.shape
    sums = [p[2] for p in PARTS]
    sent = [p[3] for p in PARTS]
    vmem = pltpu.VMEM
    scratch = (
        [vmem((2, 8, HALF + EXTRA), F32), vmem((8, HALF + EXTRA), F32)]
        + [vmem((2, SIDE, SIDE, SIDE, ROWS, w), BF16) for w in sent]
        + [
            vmem((4, 2, HALF, FFS), BF16),
            vmem((2, 2, FFS, HALF), BF16),
            vmem((4, SIDE, SIDE, SIDE, ROWS, FFS), F32),
            vmem((2, SIDE, SIDE, SIDE, ROWS, 2 * FFS), BF16),
        ]
        + [vmem((SIDE, SIDE, SIDE, ROWS, w), BF16) for w in sums]
        + [vmem((SIDE, SIDE, ROWS, w), BF16) for _ in range(3) for w in sums]
        + [vmem((SIDE, ROWS, w), BF16) for _ in range(3) for w in sums]
        + [vmem((3, ROWS, w), BF16) for w in sums]
        + [vmem((2, 8, HALF), F32), vmem((8, HALF), F32)]
        + [pltpu.SemaphoreType.DMA((N_COPIES,)), pltpu.SemaphoreType.DMA((N_COPIES,)), pltpu.SemaphoreType.DMA((9,))]
    )
    in_vmem = pl.BlockSpec(memory_space=pltpu.VMEM)
    in_hbm = pl.BlockSpec(memory_space=pl.ANY)
    return pl.pallas_call(
        kernel,
        out_shape=jax.ShapeDtypeStruct((rows, width), BF16),
        in_specs=[in_vmem] * 3 + [in_hbm] * 3,
        out_specs=in_vmem,
        scratch_shapes=scratch,
        compiler_params=pltpu.CompilerParams(
            collective_id=0, has_side_effects=True, vmem_limit_bytes=62 * 2**20
        ),
        cost_estimate=pl.CostEstimate(flops=2 * 1024 * 7168 * 1536, bytes_accessed=22 * 2**20, transcendentals=2**19),
    )(activations, expert_ids, route_weights, w_gate, w_up, w_down)


def solution(mesh):
    return jax.shard_map(
        body,
        mesh=mesh,
        in_specs=(
            P(("node", "local"), None),
            P(("node", "local"), None),
            P(("node", "local"), None),
            P("local", None, "node"),
            P("local", None, "node"),
            P("local", "node", None),
        ),
        out_specs=P(("node", "local"), None),
        check_vma=False,
    )
```

time: 743 us -> 113 us (0.15)
  waiting for transfers between devices: 551 us -> 0 us
  Pallas kernels: 0 us -> 112 us
  local copies, waits for them, and re-layouts: 57.5 us -> 1.55 us
  blocking collectives: 40.9 us -> 0 us
  matrix products: 31.1 us -> 0 us
  other arithmetic: 23.7 us -> 0 us
  starting transfers between devices: 22.3 us -> 0 us
  between operations: 13.5 us -> 0.01 us
    all_to_all x3 -> x0, waiting for transfers between devices: 514 us -> none  [the longest x1 257 us: body(): lax.all_to_all(contrib, 'local', split_axis=0, concat_axis=0, tiled=True)]
    pallas_call x0 -> x1, Pallas kernels: none -> 112 us  [body(): pl.pallas_call(kernel, out_shape=jax.ShapeDtypeStruct((rows, width), BF16...]
    all_gather x3 -> x0, blocking collectives: 40.9 us -> none  [the longest x1 15.4 us: body(): lax.all_gather(expert_ids, 'node', axis=0, tiled=True)]
    reduce_scatter x1 -> x0, waiting for transfers between devices: 36.6 us -> none  [body(): lax.psum_scatter(summed.astype(jnp.bfloat16), 'node', scatter_dimension=0...]
    gather x2 -> x0, local copies, waits for them, and re-layouts: 32.5 us -> none  [the longest x1 21.1 us: body(): returned.reshape(experts * capacity, width)[slots].astype(jnp.float32)]
    dot_general x3 -> x0, matrix products: 31.1 us -> none  [the longest x1 11.4 us: expert_apply(): jnp.einsum('secd,edf->secf', features, w_up, preferred_element_type=jnp.f...]
    all_to_all x3 -> x0, starting transfers between devices: 22.2 us -> none  [the longest x1 8.47 us: body(): lax.all_to_all(contrib, 'local', split_axis=0, concat_axis=0, tiled=True)]
    convert_element_type x1 -> x0, local copies, waits for them, and re-layouts: 13.6 us -> none  [expert_apply(): (partial_out * weights.astype(jnp.float32)[..., None]).astype(jnp.bfloat16)]
  transfers between devices with their start and end apart: 4 -> 0, of which waited for: 3 -> 0; matrix products, arithmetic and copies ran while one was open for 4% -> 0% of each run, Pallas kernels for 0% -> 0%
where the time goes in v1:
time: 113 us
  Pallas kernels  112 us (99%)
  local copies, waits for them, and re-layouts  1.55 us (1%)
    pallas_call x1, Pallas kernels, body(): pl.pallas_call(kernel, out_shape=jax.ShapeDtypeStruct((rows, width), BF16...  112 us

profile of v1, /device:TPU:1, one launch (start us, length us, event | category | flops | bytes accessed | tf_op | source)
XLA Modules:
  0.0 113.2 jit_solution(17671568019069138975)
XLA Ops:
  0.0 111.6 %shard_map.64 = bf16[8,7168]{1,0:T(8,128)(2,1)} custom-call(bf16[8,7168]{1,0:T(8,128)(2,1)} %x_in.1, s32[8,8]{1,0:T(8,128)} %ids_in.1, bf16[8,8]{1,0:T(8,128)(2,1)} %rw_in.1, bf16[2,7168,256]{2,1,0:T(8,128)(2,1)} %wg_hbm.1, bf16[2,7168,256]{2,1,0:T(8,128)(2,1)} %wu_hbm.1, bf16[2,256,7168]{2,1,0:T(8,128)(2,1)} %wd_hbm.1), custom_call_target="tpu_custom_call" | custom-call | flops 22548578304 | bytes 23068672 | tf_op jit(solution)/shard_map/pallas_call | solution.py:341
  111.6 1.6 %copy.8 = bf16[8,7168]{1,0:T(8,128)(2,1)} copy(bf16[8,7168]{1,0:T(8,128)(2,1)} %shard_map.64) | data formatting | bytes 229376

commit v2 on v1

v2 whole, which is shorter than its diff:
```python
import jax
import jax.numpy as jnp
from jax import lax
from jax.experimental import pallas as pl
from jax.experimental.pallas import tpu as pltpu
from jax.sharding import PartitionSpec as P

MESH = pl.DeviceIdType.MESH
F32 = jnp.float32
BF16 = jnp.bfloat16

SIDE = 4
ROWS = 16
HALF = 3584
EXTRA = 128
FFS = 256
PARTS = (
    ((0, 1, 2), 0, 1280, 1280),
    ((1, 2, 0), 1280, 1280, 1280),
    ((2, 0, 1), 2560, 1024, 1152),
)


def kernel(
    x_in, ids_in, rw_in, wg_hbm, wu_hbm, wd_hbm, out_ref,
    pack, pair, xb0, xb1, xb2, wgu, wd, acc, hb,
    ob0, ob1, ob2, ro0, ro1, ro2, rp0, rp1, rp2, rm0, rm1, rm2,
    bo0, bo1, bo2, bp0, bp1, bp2, bm0, bm1, bm2, ra0, ra1, ra2,
    fin, fin_got, ssem, rsem, lsem,
):
    node = lax.axis_index("node")
    local = lax.axis_index("local")
    core = lax.rem(node, 2)
    me = (local // SIDE, lax.rem(local, SIDE), node // 2)
    mate = 1 - core
    xb, ob = (xb0, xb1, xb2), (ob0, ob1, ob2)
    ro, rp, rm = (ro0, ro1, ro2), (rp0, rp1, rp2), (rm0, rm1, rm2)
    bo, bp, bm, ra = (bo0, bo1, bo2), (bp0, bp1, bp2), (bm0, bm1, bm2), (ra0, ra1, ra2)

    def off(d, k):
        return lax.rem(me[d] + k, SIDE)

    def device(d=None, k=0, other_core=False):
        at = [off(i, k) if i == d else me[i] for i in range(3)]
        return (at[2] * 2 + (mate if other_core else core), at[0] * SIDE + at[1])

    def ix(*pairs):
        at = [slice(None)] * 3
        for d, v in pairs:
            at[d] = v
        return tuple(at)

    copies, drained = [], []

    def drain(cps):
        for cp in cps:
            cp.wait_send()
            drained.append(cp)

    def send(src, dst, to):
        n = len(copies)
        cp = pltpu.make_async_remote_copy(
            src_ref=src, dst_ref=dst, send_sem=ssem.at[n], recv_sem=rsem.at[n], device_id=to, device_id_type=MESH
        )
        cp.start()
        copies.append(cp)
        return cp

    barrier = pltpu.get_barrier_semaphore()
    peers = [device(other_core=True)] + [device(d, k) for d in range(3) for k in (1, 2, 3)]
    for peer in peers:
        pl.semaphore_signal(barrier, inc=1, device_id=peer, device_id_type=MESH)

    lane = lax.broadcasted_iota(jnp.int32, (8, EXTRA), 1)
    dense = jnp.zeros((8, EXTRA), F32)
    ids = ids_in[...]
    rw = rw_in[...].astype(F32)
    for k in range(8):
        dense = dense + jnp.where(ids[:, k : k + 1] == lane, rw[:, k : k + 1], 0.0)
    pack[0, :, 0:HALF] = x_in[:, pl.ds(pl.multiple_of(mate * HALF, 128), HALF)].astype(F32)
    pack[0, :, HALF : HALF + EXTRA] = dense
    pair[core, :, 0:HALF] = x_in[:, pl.ds(pl.multiple_of(core * HALF, 128), HALF)].astype(F32)
    pair[core, :, HALF : HALF + EXTRA] = dense

    pl.semaphore_wait(barrier, len(peers))
    sister = device(other_core=True)
    swap = send(pack.at[0], pair.at[core], sister)
    swap.wait_recv()
    for p, (_, c0, _, width) in enumerate(PARTS):
        block = pair[:, :, c0 : c0 + width].reshape(ROWS, width)
        xb[p][core, me[0], me[1], me[2]] = block.astype(BF16)

    def gather(p, at, to):
        ref = xb[p].at[(core,) + at]
        return send(ref, ref, to)

    first_hop = []
    for p, ((a, b, c), *_) in enumerate(PARTS):
        at = ix((a, me[a]), (b, me[b]), (c, me[c]))
        first_hop.append([gather(p, at, device(a, k)) for k in (1, 3, 2)])

    loads = []
    for e in range(2):
        for g, w in enumerate((wg_hbm, wu_hbm)):
            for h in range(2):
                n = len(loads)
                cp = pltpu.make_async_copy(w.at[e, pl.ds(h * HALF, HALF)], wgu.at[2 * e + g, h], lsem.at[n])
                cp.start()
                loads.append(cp)
    own_cols = pl.ds(pl.multiple_of(core * HALF, 128), HALF)
    mate_cols = pl.ds(pl.multiple_of(mate * HALF, 128), HALF)
    cp = pltpu.make_async_copy(wd_hbm.at[:, :, own_cols], wd.at[core], lsem.at[len(loads)])
    cp.start()
    loads.append(cp)

    wd_cp = send(wd_hbm.at[:, :, mate_cols], wd.at[core], sister)
    acc[...] = jnp.zeros_like(acc)

    low, high = pl.ds(0, 2), pl.ds(2, 2)
    near_got = [[None] * 4 for _ in PARTS]
    far_got = [[None] * 4 for _ in PARTS]
    mate_got = [[[] for _ in range(5)] for _ in PARTS]

    def spread(p, k):
        (a, b, c), *_ = PARTS[p]
        at = ix((b, off(b, k)), (c, me[c]))
        near_got[p][k] = [gather(p, at, device(c, j)) for j in (1, 3)]

    def pass_on(p, k):
        (a, b, c), *_ = PARTS[p]
        bi = off(b, k)
        cps = []
        for cp, half, j, to in zip(near_got[p][k], (low, high), (3, 1), (1, 3)):
            cp.wait_recv()
            cps.append(gather(p, ix((a, half), (b, bi), (c, off(c, j))), device(c, to)))
            mate_got[p][k].append(gather(p, ix((b, bi), (c, off(c, j))), sister))
        far_got[p][k] = cps

    def far_to_mate(p, k):
        (a, b, c), *_ = PARTS[p]
        for cp in far_got[p][k]:
            cp.wait_recv()
        mate_got[p][k].append(gather(p, ix((b, off(b, k)), (c, off(c, 2))), sister))

    def gate_up(p, h, k):
        (_, b, c), c0, cols, _ = PARTS[p]
        if k == 4:
            lines = [ix((b, i), (c, me[c])) for i in range(SIDE)]
        else:
            lines = [ix((b, off(b, k)), (c, off(c, j))) for j in (1, 3, 2)]
        n = SIDE * ROWS
        x = jnp.concatenate([xb[p][(h,) + at + (slice(None), slice(0, cols))].reshape(n, cols) for at in lines], axis=0)
        for m in range(4):
            r = jnp.dot(x, wgu[m, h, c0 : c0 + cols], preferred_element_type=F32)
            for i, at in enumerate(lines):
                acc[(m,) + at] += r[i * n : (i + 1) * n].reshape(SIDE, ROWS, FFS)

    def own(k):
        for p in range(3):
            gate_up(p, core, k)

    def other(k):
        for p in range(3):
            for cp in mate_got[p][k]:
                cp.wait_recv()
            gate_up(p, mate, k)

    line, line_far = [], []
    for p, ((a, b, c), *_) in enumerate(PARTS):
        for cp in first_hop[p]:
            cp.wait_recv()
        at = ix((b, me[b]), (c, me[c]))
        line.append([gather(p, at, device(b, k)) for k in (1, 3)])
    for p in range(3):
        drain(line[p])
        spread(p, 0)
    for p, ((a, b, c), *_) in enumerate(PARTS):
        up, down = line[p]
        up.wait_recv()
        cps = [gather(p, ix((a, low), (b, off(b, 3)), (c, me[c])), device(b, 1))]
        down.wait_recv()
        cps.append(gather(p, ix((a, high), (b, off(b, 1)), (c, me[c])), device(b, 3)))
        line_far.append(cps)
        spread(p, 1)
    for p in range(3):
        pass_on(p, 0)
    for p, ((a, b, c), *_) in enumerate(PARTS):
        for cp in line_far[p]:
            cp.wait_recv()
        spread(p, 3)
        mate_got[p][4].append(gather(p, ix((c, me[c])), sister))
    for cp in loads:
        cp.wait()
    own(4)
    for p in range(3):
        pass_on(p, 1)
        spread(p, 2)
    other(4)
    for k, later in ((0, 3), (1, 2), (3, None), (2, None)):
        for p in range(3):
            far_to_mate(p, k)
        own(k)
        if later is not None:
            for p in range(3):
                pass_on(p, later)
        other(k)

    expert = lax.broadcasted_iota(jnp.int32, (256, EXTRA), 1) - local * 2
    hidden_cp = []
    for k in (2, 1, 3, 0):
        i = off(0, k)
        dense = xb2[core, i, :, :, :, 1024:1152].reshape(256, EXTRA).astype(F32)
        for e in range(2):
            weight = jnp.sum(jnp.where(expert == e, dense, 0.0), axis=1, keepdims=True)
            gate = acc[2 * e, i].reshape(256, FFS)
            up = acc[2 * e + 1, i].reshape(256, FFS)
            hidden = gate / (1.0 + jnp.exp(-gate)) * up * weight
            hb[core, i, :, :, :, e * FFS : (e + 1) * FFS] = hidden.astype(BF16).reshape(SIDE, SIDE, ROWS, FFS)
        hidden_cp.append(send(hb.at[core, i], hb.at[core, i], sister))
    wd_cp.wait_recv()

    def project(p, k):
        (_, b, _), c0, cols, _ = PARTS[p]
        at = ix((b, off(b, k)))

        h = jnp.concatenate([hb[(core_of,) + at].reshape(256, 2 * FFS) for core_of in range(2)], axis=1)
        for n in range(cols // 256):
            w = wd[:, :, :, c0 + n * 256 : c0 + (n + 1) * 256].reshape(4 * FFS, 256)
            r = jnp.dot(h, w, preferred_element_type=F32).astype(BF16)
            ob[p][at + (slice(None), slice(n * 256, (n + 1) * 256))] = r.reshape(SIDE, SIDE, ROWS, 256)

    def add(dst, dst_at, *others):
        total = dst[dst_at].astype(F32)
        for ref, at in others:
            total = total + ref[at].astype(F32)
        dst[dst_at] = total.astype(BF16)

    far_cp = [[None] * 4 for _ in PARTS]
    side_cp = [[[] for _ in range(4)] for _ in PARTS]

    def begin(p, k):
        (a, b, c), *_ = PARTS[p]
        project(p, k)
        bi = off(b, k)

        def to(half, s, into, j):
            return send(ob[p].at[ix((a, half), (b, bi), (c, off(c, s)))], into[p].at[bi, half], device(c, j))

        far_cp[p][k] = (to(low, 2, ro, 1), to(high, 2, ro, 3))
        side_cp[p][k] += [to(high, 1, rp, 1), to(low, 3, rm, 3)]

    def relay(p, k):
        (a, b, c), *_ = PARTS[p]
        bi = off(b, k)
        for cp, half, s, into in zip(far_cp[p][k], (low, high), (1, 3), (rp, rm)):
            cp.wait_recv()
            at = ix((a, half), (b, bi), (c, off(c, s)))
            add(ob[p], at, (ro[p], (bi, half)))
            side_cp[p][k].append(send(ob[p].at[at], into[p].at[bi, half], device(c, s)))

    def settle(p, k):
        (a, b, c), *_ = PARTS[p]
        bi = off(b, k)
        for cp in side_cp[p][k]:
            cp.wait_recv()
        add(ob[p], ix((b, bi), (c, me[c])), (rp[p], bi), (rm[p], bi))

    line_opp, line_cp = [None] * 3, [[] for _ in PARTS]

    def along_b(p, k, half, into, j):
        (a, b, c), *_ = PARTS[p]
        return send(ob[p].at[ix((a, half), (b, off(b, k)), (c, me[c]))], into[p].at[half], device(b, j))

    hidden_cp[0].wait_recv()
    begin(2, 2)
    for cp in hidden_cp[1:]:
        cp.wait_recv()
    for p in (0, 1):
        begin(p, 2)
    for p in (2, 0, 1):
        begin(p, 1)
    for p in (2, 0, 1):
        relay(p, 2)
        begin(p, 3)
    for p in (2, 0, 1):
        relay(p, 1)
        begin(p, 0)
    for p in (2, 0, 1):
        settle(p, 2)
        line_opp[p] = (along_b(p, 2, low, bo, 1), along_b(p, 2, high, bo, 3))
        relay(p, 3)
    for p in (2, 0, 1):
        relay(p, 0)
        settle(p, 1)
        line_cp[p].append(along_b(p, 1, high, bp, 1))
    for p in (2, 0, 1):
        settle(p, 3)
        line_cp[p].append(along_b(p, 3, low, bm, 3))
    for p, ((a, b, c), *_) in enumerate(PARTS):
        line_opp[p][0].wait_recv()
        add(ob[p], ix((a, low), (b, off(b, 1)), (c, me[c])), (bo[p], low))
        line_cp[p].append(along_b(p, 1, low, bp, 1))
        line_opp[p][1].wait_recv()
        add(ob[p], ix((a, high), (b, off(b, 3)), (c, me[c])), (bo[p], high))
        line_cp[p].append(along_b(p, 3, high, bm, 3))
    last = [[] for _ in PARTS]
    for p, ((a, b, c), *_) in enumerate(PARTS):
        settle(p, 0)
        for cp in line_cp[p]:
            cp.wait_recv()
        add(ob[p], ix((b, me[b]), (c, me[c])), (bp[p], slice(None)), (bm[p], slice(None)))
        for k in (1, 2, 3):
            at = ix((a, off(a, k)), (b, me[b]), (c, me[c]))
            last[p].append(send(ob[p].at[at], ra[p].at[k - 1], device(a, k)))
    for p, ((a, b, c), c0, cols, _) in enumerate(PARTS):
        total = ob[p][me].astype(F32)
        for k in (1, 2, 3):
            last[p][k - 1].wait_recv()
            total = total + ra[p][k - 1].astype(F32)
        fin[0, :, c0 : c0 + cols] = total[0:8]
        fin[1, :, c0 : c0 + cols] = total[8:16]
    final = send(fin.at[mate], fin_got, sister)
    final.wait_recv()
    first = core == 0
    mine, got = fin[core], fin_got[...]
    out_ref[:, 0:HALF] = jnp.where(first, mine, got).astype(BF16)
    out_ref[:, HALF : 2 * HALF] = jnp.where(first, got, mine).astype(BF16)
    for cp in copies:
        if not any(cp is other for other in drained):
            cp.wait_send()
    assert len(copies) == N_COPIES


N_COPIES = 214


def body(activations, expert_ids, route_weights, w_gate, w_up, w_down):
    rows, width = activations.shape
    sums = [p[2] for p in PARTS]
    sent = [p[3] for p in PARTS]
    vmem = pltpu.VMEM
    scratch = (
        [vmem((1, 8, HALF + EXTRA), F32), vmem((2, 8, HALF + EXTRA), F32)]
        + [vmem((2, SIDE, SIDE, SIDE, ROWS, w), BF16) for w in sent]
        + [
            vmem((4, 2, HALF, FFS), BF16),
            vmem((2, 2, FFS, HALF), BF16),
            vmem((4, SIDE, SIDE, SIDE, ROWS, FFS), F32),
            vmem((2, SIDE, SIDE, SIDE, ROWS, 2 * FFS), BF16),
        ]
        + [vmem((SIDE, SIDE, SIDE, ROWS, w), BF16) for w in sums]
        + [vmem((SIDE, SIDE, ROWS, w), BF16) for _ in range(3) for w in sums]
        + [vmem((SIDE, ROWS, w), BF16) for _ in range(3) for w in sums]
        + [vmem((3, ROWS, w), BF16) for w in sums]
        + [vmem((2, 8, HALF), F32), vmem((8, HALF), F32)]
        + [pltpu.SemaphoreType.DMA((N_COPIES,)), pltpu.SemaphoreType.DMA((N_COPIES,)), pltpu.SemaphoreType.DMA((9,))]
    )
    in_vmem = pl.BlockSpec(memory_space=pltpu.VMEM)
    in_hbm = pl.BlockSpec(memory_space=pl.ANY)
    return pl.pallas_call(
        kernel,
        out_shape=jax.ShapeDtypeStruct((rows, width), BF16),
        in_specs=[in_vmem] * 3 + [in_hbm] * 3,
        out_specs=in_vmem,
        scratch_shapes=scratch,
        compiler_params=pltpu.CompilerParams(
            collective_id=0, has_side_effects=True, vmem_limit_bytes=62 * 2**20
        ),
        cost_estimate=pl.CostEstimate(flops=2 * 1024 * 7168 * 1536, bytes_accessed=22 * 2**20, transcendentals=2**19),
    )(activations, expert_ids, route_weights, w_gate, w_up, w_down)


def solution(mesh):
    return jax.shard_map(
        body,
        mesh=mesh,
        in_specs=(
            P(("node", "local"), None),
            P(("node", "local"), None),
            P(("node", "local"), None),
            P("local", None, "node"),
            P("local", None, "node"),
            P("local", "node", None),
        ),
        out_specs=P(("node", "local"), None),
        check_vma=False,
    )
```

time: 113 us -> 96.1 us (0.85)
  Pallas kernels: 112 us -> 94.3 us
    pallas_call x1, Pallas kernels: 112 us -> 94.3 us  [body(): pl.pallas_call(kernel, out_shape=jax.ShapeDtypeStruct((rows, width), BF16...]
where the time goes in v2:
time: 96.1 us; the launch traced here: 95.9 us
  Pallas kernels  94.3 us (98%)
  local copies, waits for them, and re-layouts  1.55 us (2%)
    pallas_call x1, Pallas kernels, body(): pl.pallas_call(kernel, out_shape=jax.ShapeDtypeStruct((rows, width), BF16...  94.3 us

profile of v2, /device:TPU:1, one launch (start us, length us, event | category | flops | bytes accessed | tf_op | source)
XLA Modules:
  0.0 95.9 jit_solution(8236317279029810156)
XLA Ops:
  0.0 94.3 %shard_map.64 = bf16[8,7168]{1,0:T(8,128)(2,1)} custom-call(bf16[8,7168]{1,0:T(8,128)(2,1)} %x_in.1, s32[8,8]{1,0:T(8,128)} %ids_in.1, bf16[8,8]{1,0:T(8,128)(2,1)} %rw_in.1, bf16[2,7168,256]{2,1,0:T(8,128)(2,1)} %wg_hbm.1, bf16[2,7168,256]{2,1,0:T(8,128)(2,1)} %wu_hbm.1, bf16[2,256,7168]{2,1,0:T(8,128)(2,1)} %wd_hbm.1), custom_call_target="tpu_custom_call" | custom-call | flops 22548578304 | bytes 23068672 | tf_op jit(solution)/shard_map/pallas_call | solution.py:360
  94.4 1.6 %copy.8 = bf16[8,7168]{1,0:T(8,128)(2,1)} copy(bf16[8,7168]{1,0:T(8,128)(2,1)} %shard_map.64) | data formatting | bytes 229376

commit v3 on v2

--- a/solution.py
+++ b/solution.py
@@ -16,17 +16,18 @@
 FFS = 256
 PARTS = (
     ((0, 1, 2), 0, 1280, 1280),
-    ((1, 2, 0), 1280, 1280, 1280),
-    ((2, 0, 1), 2560, 1024, 1152),
+    ((1, 2, 0), 2560, 1024, 1152),
+    ((2, 0, 1), 1280, 1280, 1280),
 )
+ORDER = (0, 2, 1)
 
 
 def kernel(
-    x_in, ids_in, rw_in, wg_hbm, wu_hbm, wd_hbm, out_ref,
-    pack, pair, xb0, xb1, xb2, wgu, wd, acc, hb,
+    x_hbm, ids_hbm, rw_hbm, wg_hbm, wu_hbm, wd_hbm, out_ref,
+    x_in, ids_in, rw_in, pack, pair, xb0, xb1, xb2, wgu, wd, acc, hb,
     ob0, ob1, ob2, ro0, ro1, ro2, rp0, rp1, rp2, rm0, rm1, rm2,
     bo0, bo1, bo2, bp0, bp1, bp2, bm0, bm1, bm2, ra0, ra1, ra2,
-    fin, fin_got, ssem, rsem, lsem,
+    fin, fin_got, ssem, rsem, lsem, isem,
 ):
     node = lax.axis_index("node")
     local = lax.axis_index("local")
@@ -71,6 +72,12 @@
     for peer in peers:
         pl.semaphore_signal(barrier, inc=1, device_id=peer, device_id_type=MESH)
 
+    fetches = []
+    for n, (src, dst) in enumerate(((x_hbm, x_in), (ids_hbm, ids_in), (rw_hbm, rw_in))):
+        fetches.append(pltpu.make_async_copy(src, dst, isem.at[n]))
+        fetches[n].start()
+    for cp in fetches:
+        cp.wait()
     lane = lax.broadcasted_iota(jnp.int32, (8, EXTRA), 1)
     dense = jnp.zeros((8, EXTRA), F32)
     ids = ids_in[...]
@@ -94,10 +101,21 @@
         ref = xb[p].at[(core,) + at]
         return send(ref, ref, to)
 
-    first_hop = []
-    for p, ((a, b, c), *_) in enumerate(PARTS):
+    first_hop = [None] * 3
+    for p in ORDER:
+        (a, b, c), *_ = PARTS[p]
         at = ix((a, me[a]), (b, me[b]), (c, me[c]))
-        first_hop.append([gather(p, at, device(a, k)) for k in (1, 3, 2)])
+        first_hop[p] = [gather(p, at, device(a, k)) for k in (2, 1, 3)]
+    line, line_far = [None] * 3, [None] * 3
+    near_got = [[None] * 4 for _ in PARTS]
+    for p in ORDER:
+        (a, b, c), *_ = PARTS[p]
+        at = ix((a, me[a]), (b, me[b]), (c, me[c]))
+        line[p] = [[gather(p, at, device(b, k))] for k in (1, 3)]
+    for p in ORDER:
+        (a, b, c), *_ = PARTS[p]
+        at = ix((a, me[a]), (b, me[b]), (c, me[c]))
+        near_got[p][0] = [[gather(p, at, device(c, k))] for k in (1, 3)]
 
     loads = []
     for e in range(2):
@@ -117,21 +135,21 @@
     acc[...] = jnp.zeros_like(acc)
 
     low, high = pl.ds(0, 2), pl.ds(2, 2)
-    near_got = [[None] * 4 for _ in PARTS]
     far_got = [[None] * 4 for _ in PARTS]
     mate_got = [[[] for _ in range(5)] for _ in PARTS]
 
     def spread(p, k):
         (a, b, c), *_ = PARTS[p]
         at = ix((b, off(b, k)), (c, me[c]))
-        near_got[p][k] = [gather(p, at, device(c, j)) for j in (1, 3)]
+        near_got[p][k] = [[gather(p, at, device(c, j))] for j in (1, 3)]
 
     def pass_on(p, k):
         (a, b, c), *_ = PARTS[p]
         bi = off(b, k)
         cps = []
-        for cp, half, j, to in zip(near_got[p][k], (low, high), (3, 1), (1, 3)):
-            cp.wait_recv()
+        for got, half, j, to in zip(near_got[p][k], (low, high), (3, 1), (1, 3)):
+            for cp in got:
+                cp.wait_recv()
             cps.append(gather(p, ix((a, half), (b, bi), (c, off(c, j))), device(c, to)))
             mate_got[p][k].append(gather(p, ix((b, bi), (c, off(c, j))), sister))
         far_got[p][k] = cps
@@ -142,12 +160,9 @@
             cp.wait_recv()
         mate_got[p][k].append(gather(p, ix((b, off(b, k)), (c, off(c, 2))), sister))
 
-    def gate_up(p, h, k):
+    def gate_up(p, h, group):
         (_, b, c), c0, cols, _ = PARTS[p]
-        if k == 4:
-            lines = [ix((b, i), (c, me[c])) for i in range(SIDE)]
-        else:
-            lines = [ix((b, off(b, k)), (c, off(c, j))) for j in (1, 3, 2)]
+        lines = [ix((b, off(b, kb)), (c, off(c, kc))) for kb, kc in group]
         n = SIDE * ROWS
         x = jnp.concatenate([xb[p][(h,) + at + (slice(None), slice(0, cols))].reshape(n, cols) for at in lines], axis=0)
         for m in range(4):
@@ -155,61 +170,85 @@
             for i, at in enumerate(lines):
                 acc[(m,) + at] += r[i * n : (i + 1) * n].reshape(SIDE, ROWS, FFS)
 
-    def own(k):
-        for p in range(3):
-            gate_up(p, core, k)
-
-    def other(k):
-        for p in range(3):
-            for cp in mate_got[p][k]:
-                cp.wait_recv()
-            gate_up(p, mate, k)
-
-    line, line_far = [], []
-    for p, ((a, b, c), *_) in enumerate(PARTS):
+    def own(group):
+        for p in ORDER:
+            gate_up(p, core, group)
+
+    def other(group, arrivals):
+        for p in ORDER:
+            for k, i in arrivals:
+                mate_got[p][k][i].wait_recv()
+            gate_up(p, mate, group)
+
+    def rest_of_line(p):
+        (a, b, c), *_ = PARTS[p]
+        half = me[a] // 2
+        buddy = 4 * half + 1 - me[a]
+        rest = pl.ds(2 - 2 * half, 2)
+        return [ix((a, i), (b, me[b]), (c, me[c])) for i in (buddy, rest)]
+
+    for p in ORDER:
+        (a, b, c), *_ = PARTS[p]
         for cp in first_hop[p]:
             cp.wait_recv()
-        at = ix((b, me[b]), (c, me[c]))
-        line.append([gather(p, at, device(b, k)) for k in (1, 3)])
-    for p in range(3):
-        drain(line[p])
-        spread(p, 0)
-    for p, ((a, b, c), *_) in enumerate(PARTS):
+        for cps, k in zip(line[p], (1, 3)):
+            cps += [gather(p, at, device(b, k)) for at in rest_of_line(p)]
+    for p in ORDER:
+        drain(line[p][0] + line[p][1])
+        for cps, k in zip(near_got[p][0], (1, 3)):
+            cps += [gather(p, at, device(PARTS[p][0][2], k)) for at in rest_of_line(p)]
+    for p in ORDER:
+        (a, b, c), *_ = PARTS[p]
         up, down = line[p]
-        up.wait_recv()
+        for cp in up:
+            cp.wait_recv()
         cps = [gather(p, ix((a, low), (b, off(b, 3)), (c, me[c])), device(b, 1))]
-        down.wait_recv()
+        for cp in down:
+            cp.wait_recv()
         cps.append(gather(p, ix((a, high), (b, off(b, 1)), (c, me[c])), device(b, 3)))
-        line_far.append(cps)
+        line_far[p] = cps
         spread(p, 1)
-    for p in range(3):
+    for p in ORDER:
         pass_on(p, 0)
-    for p, ((a, b, c), *_) in enumerate(PARTS):
+    for p in ORDER:
+        (a, b, c), *_ = PARTS[p]
         for cp in line_far[p]:
             cp.wait_recv()
         spread(p, 3)
         mate_got[p][4].append(gather(p, ix((c, me[c])), sister))
     for cp in loads:
         cp.wait()
-    own(4)
-    for p in range(3):
+    plane = [(k, 0) for k in range(SIDE)]
+    own(plane)
+    for p in ORDER:
         pass_on(p, 1)
         spread(p, 2)
-    other(4)
-    for k, later in ((0, 3), (1, 2), (3, None), (2, None)):
-        for p in range(3):
+    other(plane, [(4, 0)])
+    for k, later in ((0, 3), (1, 2)):
+        group = [(k, 1), (k, 3), (k, 2)]
+        for p in ORDER:
             far_to_mate(p, k)
-        own(k)
-        if later is not None:
-            for p in range(3):
-                pass_on(p, later)
-        other(k)
+        own(group)
+        for p in ORDER:
+            pass_on(p, later)
+        other(group, [(k, 0), (k, 1), (k, 2)])
+    group = [(3, 1), (3, 3), (2, 1), (2, 3)]
+    own(group)
+    for p in ORDER:
+        far_to_mate(p, 3)
+    other(group, [(3, 0), (3, 1), (2, 0), (2, 1)])
+    for p in ORDER:
+        far_to_mate(p, 2)
+    group = [(3, 2), (2, 2)]
+    own(group)
+    other(group, [(3, 2), (2, 2)])
 
     expert = lax.broadcasted_iota(jnp.int32, (256, EXTRA), 1) - local * 2
     hidden_cp = []
-    for k in (2, 1, 3, 0):
+
+    def hide(k):
         i = off(0, k)
-        dense = xb2[core, i, :, :, :, 1024:1152].reshape(256, EXTRA).astype(F32)
+        dense = xb1[core, i, :, :, :, 1024:1152].reshape(256, EXTRA).astype(F32)
         for e in range(2):
             weight = jnp.sum(jnp.where(expert == e, dense, 0.0), axis=1, keepdims=True)
             gate = acc[2 * e, i].reshape(256, FFS)
@@ -217,7 +256,6 @@
             hidden = gate / (1.0 + jnp.exp(-gate)) * up * weight
             hb[core, i, :, :, :, e * FFS : (e + 1) * FFS] = hidden.astype(BF16).reshape(SIDE, SIDE, ROWS, FFS)
         hidden_cp.append(send(hb.at[core, i], hb.at[core, i], sister))
-    wd_cp.wait_recv()
 
     def project(p, k):
         (_, b, _), c0, cols, _ = PARTS[p]
@@ -271,8 +309,12 @@
         (a, b, c), *_ = PARTS[p]
         return send(ob[p].at[ix((a, half), (b, off(b, k)), (c, me[c]))], into[p].at[half], device(b, j))
 
+    for k in (2, 1, 3):
+        hide(k)
+    wd_cp.wait_recv()
     hidden_cp[0].wait_recv()
     begin(2, 2)
+    hide(0)
     for cp in hidden_cp[1:]:
         cp.wait_recv()
     for p in (0, 1):
@@ -331,7 +373,7 @@
     assert len(copies) == N_COPIES
 
 
-N_COPIES = 214
+N_COPIES = 238
 
 
 def body(activations, expert_ids, route_weights, w_gate, w_up, w_down):
@@ -340,7 +382,7 @@
     sent = [p[3] for p in PARTS]
     vmem = pltpu.VMEM
     scratch = (
-        [vmem((1, 8, HALF + EXTRA), F32), vmem((2, 8, HALF + EXTRA), F32)]
+        [vmem((rows, width), BF16), vmem((8, 8), jnp.int32), vmem((8, 8), BF16), vmem((1, 8, HALF + EXTRA), F32), vmem((2, 8, HALF + EXTRA), F32)]
         + [vmem((2, SIDE, SIDE, SIDE, ROWS, w), BF16) for w in sent]
         + [
             vmem((4, 2, HALF, FFS), BF16),
@@ -353,14 +395,14 @@
         + [vmem((SIDE, ROWS, w), BF16) for _ in range(3) for w in sums]
         + [vmem((3, ROWS, w), BF16) for w in sums]
         + [vmem((2, 8, HALF), F32), vmem((8, HALF), F32)]
-        + [pltpu.SemaphoreType.DMA((N_COPIES,)), pltpu.SemaphoreType.DMA((N_COPIES,)), pltpu.SemaphoreType.DMA((9,))]
+        + [pltpu.SemaphoreType.DMA((N_COPIES,)), pltpu.SemaphoreType.DMA((N_COPIES,)), pltpu.SemaphoreType.DMA((9,)), pltpu.SemaphoreType.DMA((3,))]
     )
     in_vmem = pl.BlockSpec(memory_space=pltpu.VMEM)
     in_hbm = pl.BlockSpec(memory_space=pl.ANY)
     return pl.pallas_call(
         kernel,
         out_shape=jax.ShapeDtypeStruct((rows, width), BF16),
-        in_specs=[in_vmem] * 3 + [in_hbm] * 3,
+        in_specs=[in_hbm] * 6,
         out_specs=in_vmem,
         scratch_shapes=scratch,
         compiler_params=pltpu.CompilerParams(

time: 96.1 us -> 92.9 us (0.967)
  Pallas kernels: 94.3 us -> 91.2 us
    pallas_call x1, Pallas kernels: 94.3 us -> 91.2 us  [body(): pl.pallas_call(kernel, out_shape=jax.ShapeDtypeStruct((rows, width), BF16...]
where the time goes in v3:
time: 92.9 us; the launch traced here: 92.7 us
  Pallas kernels  91.2 us (98%)
  local copies, waits for them, and re-layouts  1.55 us (2%)
    pallas_call x1, Pallas kernels, body(): pl.pallas_call(kernel, out_shape=jax.ShapeDtypeStruct((rows, width), BF16...  91.2 us

profile of v3, /device:TPU:1, one launch (start us, length us, event | category | flops | bytes accessed | tf_op | source)
XLA Modules:
  0.0 92.7 jit_solution(15304531025512242710)
XLA Ops:
  0.0 91.2 %shard_map.64 = bf16[8,7168]{1,0:T(8,128)(2,1)} custom-call(bf16[8,7168]{1,0:T(8,128)(2,1)} %x_hbm.1, s32[8,8]{1,0:T(8,128)} %ids_hbm.1, bf16[8,8]{1,0:T(8,128)(2,1)} %rw_hbm.1, bf16[2,7168,256]{2,1,0:T(8,128)(2,1)} %wg_hbm.1, bf16[2,7168,256]{2,1,0:T(8,128)(2,1)} %wu_hbm.1, bf16[2,256,7168]{2,1,0:T(8,128)(2,1)} %wd_hbm.1), custom_call_target="tpu_custom_call" | custom-call | flops 22548578304 | bytes 23068672 | tf_op jit(solution)/shard_map/pallas_call | solution.py:402
  91.2 1.6 %copy.8 = bf16[8,7168]{1,0:T(8,128)(2,1)} copy(bf16[8,7168]{1,0:T(8,128)(2,1)} %shard_map.64) | data formatting | bytes 229376

commit v4 on v3

--- a/solution.py
+++ b/solution.py
@@ -55,8 +55,9 @@
 
     def drain(cps):
         for cp in cps:
-            cp.wait_send()
-            drained.append(cp)
+            if not any(cp is other for other in drained):
+                cp.wait_send()
+                drained.append(cp)
 
     def send(src, dst, to):
         n = len(copies)
@@ -194,7 +195,6 @@
         for cps, k in zip(line[p], (1, 3)):
             cps += [gather(p, at, device(b, k)) for at in rest_of_line(p)]
     for p in ORDER:
-        drain(line[p][0] + line[p][1])
         for cps, k in zip(near_got[p][0], (1, 3)):
             cps += [gather(p, at, device(PARTS[p][0][2], k)) for at in rest_of_line(p)]
     for p in ORDER:
@@ -245,6 +245,7 @@
 
     expert = lax.broadcasted_iota(jnp.int32, (256, EXTRA), 1) - local * 2
     hidden_cp = []
+    gathered = list(copies)
 
     def hide(k):
         i = off(0, k)
@@ -257,15 +258,18 @@
             hb[core, i, :, :, :, e * FFS : (e + 1) * FFS] = hidden.astype(BF16).reshape(SIDE, SIDE, ROWS, FFS)
         hidden_cp.append(send(hb.at[core, i], hb.at[core, i], sister))
 
-    def project(p, k):
-        (_, b, _), c0, cols, _ = PARTS[p]
-        at = ix((b, off(b, k)))
-
-        h = jnp.concatenate([hb[(core_of,) + at].reshape(256, 2 * FFS) for core_of in range(2)], axis=1)
-        for n in range(cols // 256):
-            w = wd[:, :, :, c0 + n * 256 : c0 + (n + 1) * 256].reshape(4 * FFS, 256)
+    def project(p, k, places):
+        (_, b, c), c0, cols, _ = PARTS[p]
+        lines = [ix((b, off(b, k)), (c, off(c, j))) for j in places]
+        n = SIDE * ROWS
+        h = jnp.concatenate(
+            [jnp.concatenate([hb[(i,) + at].reshape(n, 2 * FFS) for i in range(2)], axis=1) for at in lines], axis=0
+        )
+        for i in range(cols // 256):
+            w = wd[:, :, :, c0 + i * 256 : c0 + (i + 1) * 256].reshape(4 * FFS, 256)
             r = jnp.dot(h, w, preferred_element_type=F32).astype(BF16)
-            ob[p][at + (slice(None), slice(n * 256, (n + 1) * 256))] = r.reshape(SIDE, SIDE, ROWS, 256)
+            for j, at in enumerate(lines):
+                ob[p][at + (slice(None), slice(i * 256, (i + 1) * 256))] = r[j * n : (j + 1) * n].reshape(SIDE, ROWS, 256)
 
     def add(dst, dst_at, *others):
         total = dst[dst_at].astype(F32)
@@ -276,16 +280,18 @@
     far_cp = [[None] * 4 for _ in PARTS]
     side_cp = [[[] for _ in range(4)] for _ in PARTS]
 
-    def begin(p, k):
-        (a, b, c), *_ = PARTS[p]
-        project(p, k)
+    def begin(p, k, stage=2):
+        (a, b, c), *_ = PARTS[p]
+        project(p, k, ((2, 0), (1, 3), (2, 1, 3, 0))[stage])
         bi = off(b, k)
 
         def to(half, s, into, j):
             return send(ob[p].at[ix((a, half), (b, bi), (c, off(c, s)))], into[p].at[bi, half], device(c, j))
 
-        far_cp[p][k] = (to(low, 2, ro, 1), to(high, 2, ro, 3))
-        side_cp[p][k] += [to(high, 1, rp, 1), to(low, 3, rm, 3)]
+        if stage != 1:
+            far_cp[p][k] = (to(low, 2, ro, 1), to(high, 2, ro, 3))
+        if stage != 0:
+            side_cp[p][k] += [to(high, 1, rp, 1), to(low, 3, rm, 3)]
 
     def relay(p, k):
         (a, b, c), *_ = PARTS[p]
@@ -313,12 +319,14 @@
         hide(k)
     wd_cp.wait_recv()
     hidden_cp[0].wait_recv()
-    begin(2, 2)
+    begin(2, 2, 0)
     hide(0)
     for cp in hidden_cp[1:]:
         cp.wait_recv()
     for p in (0, 1):
-        begin(p, 2)
+        begin(p, 2, 0)
+    for p in (2, 0, 1):
+        begin(p, 2, 1)
     for p in (2, 0, 1):
         begin(p, 1)
     for p in (2, 0, 1):
@@ -327,18 +335,20 @@
     for p in (2, 0, 1):
         relay(p, 1)
         begin(p, 0)
+    drain(gathered)
     for p in (2, 0, 1):
         settle(p, 2)
         line_opp[p] = (along_b(p, 2, low, bo, 1), along_b(p, 2, high, bo, 3))
         relay(p, 3)
     for p in (2, 0, 1):
-        relay(p, 0)
         settle(p, 1)
         line_cp[p].append(along_b(p, 1, high, bp, 1))
+        relay(p, 0)
     for p in (2, 0, 1):
         settle(p, 3)
         line_cp[p].append(along_b(p, 3, low, bm, 3))
-    for p, ((a, b, c), *_) in enumerate(PARTS):
+    for p in (2, 0, 1):
+        (a, b, c), *_ = PARTS[p]
         line_opp[p][0].wait_recv()
         add(ob[p], ix((a, low), (b, off(b, 1)), (c, me[c])), (bo[p], low))
         line_cp[p].append(along_b(p, 1, low, bp, 1))
@@ -346,30 +356,36 @@
         add(ob[p], ix((a, high), (b, off(b, 3)), (c, me[c])), (bo[p], high))
         line_cp[p].append(along_b(p, 3, high, bm, 3))
     last = [[] for _ in PARTS]
-    for p, ((a, b, c), *_) in enumerate(PARTS):
-        settle(p, 0)
-        for cp in line_cp[p]:
-            cp.wait_recv()
-        add(ob[p], ix((b, me[b]), (c, me[c])), (bp[p], slice(None)), (bm[p], slice(None)))
-        for k in (1, 2, 3):
+    for p in (2, 0, 1):
+        (a, b, c), *_ = PARTS[p]
+        for cp in side_cp[p][0] + line_cp[p]:
+            cp.wait_recv()
+        every = slice(None)
+        add(
+            ob[p], ix((b, me[b]), (c, me[c])),
+            (rp[p], me[b]), (rm[p], me[b]), (bp[p], every), (bm[p], every),
+        )
+        for k in (2, 1, 3):
             at = ix((a, off(a, k)), (b, me[b]), (c, me[c]))
             last[p].append(send(ob[p].at[at], ra[p].at[k - 1], device(a, k)))
-    for p, ((a, b, c), c0, cols, _) in enumerate(PARTS):
+    drain([cp for cp in copies if not any(cp is other for cps in last for other in cps)])
+    for p in (2, 0, 1):
+        _, c0, cols, _ = PARTS[p]
         total = ob[p][me].astype(F32)
-        for k in (1, 2, 3):
-            last[p][k - 1].wait_recv()
-            total = total + ra[p][k - 1].astype(F32)
+        for cp in last[p]:
+            cp.wait_recv()
+        for k in range(3):
+            total = total + ra[p][k].astype(F32)
         fin[0, :, c0 : c0 + cols] = total[0:8]
         fin[1, :, c0 : c0 + cols] = total[8:16]
     final = send(fin.at[mate], fin_got, sister)
+    drain([cp for cps in last for cp in cps])
     final.wait_recv()
     first = core == 0
     mine, got = fin[core], fin_got[...]
     out_ref[:, 0:HALF] = jnp.where(first, mine, got).astype(BF16)
     out_ref[:, HALF : 2 * HALF] = jnp.where(first, got, mine).astype(BF16)
-    for cp in copies:
-        if not any(cp is other for other in drained):
-            cp.wait_send()
+    drain(copies)
     assert len(copies) == N_COPIES
 
 

time: 92.9 us -> 91.8 us (0.988)
  Pallas kernels: 91.2 us -> 90.1 us
    pallas_call x1, Pallas kernels: 91.2 us -> 90.1 us  [body(): pl.pallas_call(kernel, out_shape=jax.ShapeDtypeStruct((rows, width), BF16...]
where the time goes in v4:
time: 91.8 us; the launch traced here: 91.6 us
  Pallas kernels  90.1 us (98%)
  local copies, waits for them, and re-layouts  1.55 us (2%)
    pallas_call x1, Pallas kernels, body(): pl.pallas_call(kernel, out_shape=jax.ShapeDtypeStruct((rows, width), BF16...  90.1 us

profile of v4, /device:TPU:1, one launch (start us, length us, event | category | flops | bytes accessed | tf_op | source)
XLA Modules:
  0.0 91.6 jit_solution(970298605911193621)
XLA Ops:
  0.0 90.1 %shard_map.64 = bf16[8,7168]{1,0:T(8,128)(2,1)} custom-call(bf16[8,7168]{1,0:T(8,128)(2,1)} %x_hbm.1, s32[8,8]{1,0:T(8,128)} %ids_hbm.1, bf16[8,8]{1,0:T(8,128)(2,1)} %rw_hbm.1, bf16[2,7168,256]{2,1,0:T(8,128)(2,1)} %wg_hbm.1, bf16[2,7168,256]{2,1,0:T(8,128)(2,1)} %wu_hbm.1, bf16[2,256,7168]{2,1,0:T(8,128)(2,1)} %wd_hbm.1), custom_call_target="tpu_custom_call" | custom-call | flops 22548578304 | bytes 23068672 | tf_op jit(solution)/shard_map/pallas_call | solution.py:418
  90.1 1.6 %copy.8 = bf16[8,7168]{1,0:T(8,128)(2,1)} copy(bf16[8,7168]{1,0:T(8,128)(2,1)} %shard_map.64) | data formatting | bytes 229376
